TPU v7x, 32 devices: a whole 2x2x4 slice. The times are simulated.
32 devices in a mesh: sample: 4 (over y, core), solver: 8 (over z, x).
Axes of the slice: x: 2, y: 2, z: 4, core: 2. Of those that a mesh axis runs over, the one named last changes fastest.
Arguments:
- other_index: int32 [11, 8192], P(None, ('sample', 'solver')), may hold values from 0 to 255
- slice_index: int32 [8192, 1], P(('sample', 'solver')), may hold values from 0 to 127; in each aligned block of 256 rows (0 to 255, 256 to 511, ...) at most 4 rows name the same one
- observed: bfloat16 [8192], P(('sample', 'solver')), may hold values from -6 to 6
- left_first: bfloat16 [256, 32], replicated, may hold values from -1 to 1
- left_cores: bfloat16 [4, 256, 32, 32], replicated, may hold values from -1 to 1
- right_cores: bfloat16 [5, 256, 32, 32], replicated, may hold values from -1 to 1
- right_last: bfloat16 [256, 32], replicated, may hold values from -1 to 1
Outputs:
- new_core: float32 [128, 1024], P(('sample', 'solver'))
- misfit: float32 [8192], P(('sample', 'solver'))
Inputs may be any that keep to these rules, and one draw needn't show every extreme that they name: `slice_index`: within each device's aligned block of 256 entries no mode-6 value appears more than 4 times, and some value appears exactly 4 times.
All inputs are finite; a program needn't handle non-finite values.
Results may differ from a plain program's by a relative error of at most 0.0048.
Values may be sent and summed in bfloat16 or wider, within the bound.
A program may use at most 192 MiB of HBM per device.

v0:
```python
import jax
import jax.numpy as jnp
from jax import lax
from jax.sharding import PartitionSpec as P

SLICES = 128


ridge_weight = 2.0


def interfaces(index_block, left_first, left_cores, right_cores, right_last):
    left = jnp.take(left_first, index_block[0], axis=0).astype(jnp.float32)
    for level in range(left_cores.shape[0]):
        mats = jnp.take(left_cores[level], index_block[level + 1], axis=0)
        left = jnp.einsum(
            "ej,ejk->ek",
            left,
            mats,
            precision=lax.Precision.HIGHEST,
            preferred_element_type=jnp.float32,
        )
    count_left = left_cores.shape[0]
    right = jnp.take(right_last, index_block[-1], axis=0).astype(jnp.float32)
    for level in range(right_cores.shape[0] - 1, -1, -1):
        mats = jnp.take(right_cores[level], index_block[count_left + 1 + level], axis=0)
        right = jnp.einsum(
            "ejk,ek->ej",
            mats,
            right,
            precision=lax.Precision.HIGHEST,
            preferred_element_type=jnp.float32,
        )
    return (left.astype(jnp.bfloat16), right.astype(jnp.bfloat16))


def outer_rows(left, right, rank):
    prod = left.astype(jnp.float32)[..., :, None] * right.astype(jnp.float32)[..., None, :]
    return prod.reshape(left.shape[:-1] + (rank * rank,)).astype(jnp.bfloat16)


def solve_group(rows, weights):
    width = rows.shape[-1]
    gram = jnp.einsum("pjcf,pjcg->jfg", rows, rows, preferred_element_type=jnp.float32)
    rhs = jnp.einsum("pjcf,pjc->jf", rows, weights, preferred_element_type=jnp.float32)
    system = gram + ridge_weight * jnp.eye(width, dtype=jnp.float32)
    chol = jnp.linalg.cholesky(system)
    half = lax.linalg.triangular_solve(chol, rhs[..., None], left_side=True, lower=True)
    solved = lax.linalg.triangular_solve(chol, half, left_side=True, lower=True, transpose_a=True)[
        ..., 0
    ]
    preds = jnp.einsum(
        "pjcf,jf->jpc",
        rows,
        solved,
        precision=lax.Precision.HIGHEST,
        preferred_element_type=jnp.float32,
    )
    return (solved, preds)


def per_device(other_index, slice_index, observed, left_first, left_cores, right_cores, right_last):
    rank = left_first.shape[1]
    values = SLICES
    count = observed.shape[0]
    devices = lax.axis_size(("sample", "solver"))
    owned = values // devices
    capacity = max(4, 2 * count // values)
    left, right = interfaces(other_index, left_first, left_cores, right_cores, right_last)
    rows = outer_rows(left, right, rank)
    ids = slice_index[:, 0]
    order = jnp.argsort(ids, stable=True)
    counts = jnp.sum(
        (ids[None, :] == jnp.arange(values, dtype=jnp.int32)[:, None]).astype(jnp.int32), axis=1
    )
    starts = jnp.cumsum(counts) - counts
    sorted_ids = ids[order]
    rank_sorted = jnp.arange(count, dtype=jnp.int32) - starts[sorted_ids]
    slot = jnp.zeros((count,), jnp.int32).at[order].set(rank_sorted)
    position = ids * capacity + slot
    value_buffer = jnp.zeros((values * capacity,), jnp.bfloat16).at[position].set(observed)
    value_buffer = value_buffer.reshape(devices, owned, capacity)
    row_buffer = jnp.zeros((values * capacity, rank * rank), jnp.bfloat16).at[position].set(rows)
    row_buffer = row_buffer.reshape(devices, owned, capacity, rank * rank)
    solved, preds = solve_group(
        lax.all_to_all(row_buffer, ("sample", "solver"), split_axis=0, concat_axis=0, tiled=True),
        lax.all_to_all(value_buffer, ("sample", "solver"), split_axis=0, concat_axis=0, tiled=True),
    )
    whole_core = lax.all_gather(solved, ("sample", "solver"), axis=0, tiled=True)
    picked = jnp.take(whole_core, ids, axis=0)
    predicted = jnp.einsum(
        "ef,ef->e",
        rows,
        picked,
        precision=lax.Precision.HIGHEST,
        preferred_element_type=jnp.float32,
    )
    misfit = observed.astype(jnp.float32) - predicted
    return (solved, misfit)


def solution(mesh):
    return jax.shard_map(
        per_device,
        mesh=mesh,
        in_specs=(
            P(None, ("sample", "solver")),
            P(("sample", "solver"), None),
            P(("sample", "solver")),
            P(),
            P(),
            P(),
            P(),
        ),
        out_specs=(P(("sample", "solver"), None), P(("sample", "solver"))),
        check_vma=False,
    )
```

profile of v0, /device:TPU:0, one launch (start us, length us, event | category | flops | bytes accessed | tf_op | source)
XLA Modules:
  0.0 1411.9 jit_solution(13339744966146509114)
XLA Ops:
  133.5 21.3 %all-to-all-done = bf16[32,4,4,1024]{3,2,1,0:T(4,128)(2,1)} async-done(((bf16[32,4,4,1024]{3,2,1,0:T(4,128)(2,1)}), bf16[32,4,4,1024]{3,2,1,0:T(4,128)(2,1)}, u32[]{:S(2)}, u32[]{:S(2)}) %all-to-all-start) | async-done | bytes 1048608 | tf_op jit(solution)/shard_map/all_to_all | solution.py:86
  156.7 10.0 convolution_bitcast_fusion
  166.7 16.4 %copy.133 = f32[4,1024,1024]{1,2,0:T(8,128)} copy(f32[4,1024,1024]{2,1,0:T(8,128)} %convolution_bitcast_fusion) | data formatting | bytes 33554432 | tf_op jit(solution)/shard_map/pjcf,pjcg->jfg/dot_general | solution.py:44
  183.1 14.4 %fusion.1 = f32[4,1024,1024]{2,1,0:T(8,128)S(1)} fusion(f32[4,1024,1024]{1,2,0:T(8,128)} %copy.133, f32[4,1024,1024]{2,1,0:T(8,128)} %convolution_bitcast_fusion, f32[1024,1024]{1,0:T(8,128)} %get-tuple-element.115, f32[1024,1024]{1,0:T(8,128)} %get-tuple-element.114), kind=kLoop, calls=%fused_computation.21 | loop fusion | flops 16777216 | bytes 58720256 | tf_op jit(solution)/shard_map/jit(cholesky)/div | solution.py:47
  203.4 46.9 %custom-call.72 = f32[4,128,128]{2,1,0:T(8,128)S(1)} custom-call(f32[4,128,128]{2,1,0:T(8,128)S(1)} %cholesky.578), custom_call_target="Cholesky" | custom-call | tf_op jit(solution)/shard_map/jit(cholesky)/cholesky | solution.py:47
  250.3 7.9 cholesky.253
  258.1 39.5 %custom-call.73 = f32[4,1,128,128]{2,3,1,0:T(8,128)S(1)} custom-call(f32[4,1,128,128]{3,2,1,0:T(8,128)S(1)} %select_bitcast_fusion.6), custom_call_target="InvertDiagBlocksLowerTriangular" | custom-call | tf_op jit(solution)/shard_map/jit(cholesky)/cholesky | solution.py:47
  306.0 47.7 %custom-call.74 = f32[4,128,128]{2,1,0:T(8,128)S(1)} custom-call(f32[4,128,128]{2,1,0:T(8,128)} %cholesky.582), custom_call_target="Cholesky" | custom-call | tf_op jit(solution)/shard_map/jit(cholesky)/cholesky | solution.py:47
  354.6 40.9 %custom-call.75 = f32[4,1,128,128]{2,3,1,0:T(8,128)} custom-call(f32[4,1,128,128]{3,2,1,0:T(8,128)} %get-tuple-element.54), custom_call_target="InvertDiagBlocksLowerTriangular" | custom-call | tf_op jit(solution)/shard_map/jit(cholesky)/cholesky | solution.py:47
  405.2 47.7 %custom-call.76 = f32[4,128,128]{2,1,0:T(8,128)S(1)} custom-call(f32[4,128,128]{2,1,0:T(8,128)} %cholesky.587), custom_call_target="Cholesky" | custom-call | tf_op jit(solution)/shard_map/jit(cholesky)/cholesky | solution.py:47
  453.8 41.1 %custom-call.77 = f32[4,1,128,128]{2,3,1,0:T(8,128)} custom-call(f32[4,1,128,128]{3,2,1,0:T(8,128)} %get-tuple-element.52), custom_call_target="InvertDiagBlocksLowerTriangular" | custom-call | tf_op jit(solution)/shard_map/jit(cholesky)/cholesky | solution.py:47
  505.3 47.7 %custom-call.78 = f32[4,128,128]{2,1,0:T(8,128)S(1)} custom-call(f32[4,128,128]{2,1,0:T(8,128)} %cholesky.592), custom_call_target="Cholesky" | custom-call | tf_op jit(solution)/shard_map/jit(cholesky)/cholesky | solution.py:47
  553.9 40.9 %custom-call.79 = f32[4,1,128,128]{2,3,1,0:T(8,128)} custom-call(f32[4,1,128,128]{3,2,1,0:T(8,128)} %get-tuple-element.50), custom_call_target="InvertDiagBlocksLowerTriangular" | custom-call | tf_op jit(solution)/shard_map/jit(cholesky)/cholesky | solution.py:47
  605.0 47.7 %custom-call.80 = f32[4,128,128]{2,1,0:T(8,128)S(1)} custom-call(f32[4,128,128]{2,1,0:T(8,128)} %cholesky.597), custom_call_target="Cholesky" | custom-call | tf_op jit(solution)/shard_map/jit(cholesky)/cholesky | solution.py:47
  653.6 40.9 %custom-call.81 = f32[4,1,128,128]{2,3,1,0:T(8,128)} custom-call(f32[4,1,128,128]{3,2,1,0:T(8,128)} %get-tuple-element.48), custom_call_target="InvertDiagBlocksLowerTriangular" | custom-call | tf_op jit(solution)/shard_map/jit(cholesky)/cholesky | solution.py:47
  704.2 47.7 %custom-call.82 = f32[4,128,128]{2,1,0:T(8,128)S(1)} custom-call(f32[4,128,128]{2,1,0:T(8,128)} %cholesky.602), custom_call_target="Cholesky" | custom-call | tf_op jit(solution)/shard_map/jit(cholesky)/cholesky | solution.py:47
  752.7 41.1 %custom-call.83 = f32[4,1,128,128]{2,3,1,0:T(8,128)} custom-call(f32[4,1,128,128]{3,2,1,0:T(8,128)} %get-tuple-element.46), custom_call_target="InvertDiagBlocksLowerTriangular" | custom-call | tf_op jit(solution)/shard_map/jit(cholesky)/cholesky | solution.py:47
  802.3 47.7 %custom-call.84 = f32[4,128,128]{2,1,0:T(8,128)S(1)} custom-call(f32[4,128,128]{2,1,0:T(8,128)} %cholesky.607), custom_call_target="Cholesky" | custom-call | tf_op jit(solution)/shard_map/jit(cholesky)/cholesky | solution.py:47
  850.9 40.7 %custom-call.85 = f32[4,1,128,128]{2,3,1,0:T(8,128)} custom-call(f32[4,1,128,128]{3,2,1,0:T(8,128)} %get-tuple-element.44), custom_call_target="InvertDiagBlocksLowerTriangular" | custom-call | tf_op jit(solution)/shard_map/jit(cholesky)/cholesky | solution.py:47
  897.8 47.1 %custom-call.86 = f32[4,128,128]{2,1,0:T(8,128)S(1)} custom-call(f32[4,128,128]{2,1,0:T(8,128)S(1)} %fusion.79), custom_call_target="Cholesky" | custom-call | tf_op jit(solution)/shard_map/jit(cholesky)/cholesky | solution.py:47
  946.7 12.7 select_select_fusion
  959.4 29.7 %while.1 = (s32[]{:T(128)}, f32[4,1024,1024]{2,1,0:T(8,128)}, s32[8,2]{0,1:T(2,128)S(1)}, f32[8,4,128,128]{3,2,0,1:T(8,128)}, s32[]{:T(128)}) while((s32[]{:T(128)}, f32[4,1024,1024]{2,1,0:T(8,128)}, s32[8,2]{0,1:T(2,128)S(1)}, f32[8,4,128,128]{3,2,0,1:T(8,128)}, s32[]{:T(128)}) %tuple.84), condition=%wide.while_cond, body=%wide.while_body.sunk | while | flops 2 | bytes 525421 | solution.py:49
  989.1 315.3 %custom-call.87 = f32[4,8,128,128]{2,3,1,0:T(8,128)S(1)} custom-call(f32[4,8,128,128]{3,2,1,0:T(8,128)} %bitcast.488), custom_call_target="InvertDiagBlocksLowerTriangular" | custom-call | tf_op jit(solution)/shard_map/triangular_solve | solution.py:49
  1342.7 66.8 %all-gather = f32[128,1024,1]{1,2,0:T(1,128)S(1)} all-gather(f32[4,1024,1]{1,2,0:T(1,128)S(1)} %constant_dynamic-update-slice_fusion.36), channel_id=2, replica_groups=mesh['sample'=4,'solver'=8] {'sample','solver'}, dimensions={0}, use_global_device_ids=true | all-gather | bytes 540672 | tf_op jit(solution)/shard_map/all_gather | solution.py:89
  (279 shorter events, 279.9 us)
Async XLA Ops:
  0.6 11.4 copy-start
  0.6 11.4 copy-start.16
  14.9 105.8 %all-to-all-start.1 = ((bf16[32,4,4]{2,1,0:T(4,128)(2,1)}), bf16[32,4,4]{2,1,0:T(4,128)(2,1)S(1)}, u32[]{:S(2)}, u32[]{:S(2)}) async-start(bf16[32,4,4]{2,1,0:T(4,128)(2,1)} %reshape.321), calls=%async_computation.1 | async-start | bytes 65536 | tf_op jit(solution)/shard_map/all_to_all | solution.py:87
  25.5 3.8 copy-start.14
  52.2 4.0 copy-start.2
  58.4 3.9 copy-start.5
  62.3 2.5 copy-start.9
  64.8 3.5 copy-start.8
  68.2 3.5 copy-start.7
  71.7 3.4 copy-start.6
  75.1 3.7 copy-start.13
  80.0 4.6 copy-start.15
  103.0 3.9 copy-start.3
  109.1 2.5 copy-start.12
  111.6 1.9 copy-start.11
  113.4 1.9 copy-start.10
  120.8 34.0 %all-to-all-start = ((bf16[32,4,4,1024]{3,2,1,0:T(4,128)(2,1)}), bf16[32,4,4,1024]{3,2,1,0:T(4,128)(2,1)}, u32[]{:S(2)}, u32[]{:S(2)}) async-start(bf16[32,4,4,1024]{3,2,1,0:T(4,128)(2,1)} %reshape.320), calls=%async_computation | async-start | bytes 2097152 | tf_op jit(solution)/shard_map/all_to_all | solution.py:86
  197.6 5.7 copy-start.1
  1409.6 1.2 copy-start.4
where the time goes:
time: 1420 us; the launch traced here: 1410 us
  other arithmetic  1030 us (73%)
  local copies, waits for them, and re-layouts  150 us (11%)
  matrix products  132 us (9%)
  blocking collectives  66.8 us (5%)
  waiting for transfers between devices  21.3 us (2%)
    another operation x34, other arithmetic, solve_group(): chol = jnp.linalg.cholesky(system)  672 us
    another operation x11, other arithmetic, solve_group(): lax.linalg.triangular_solve(chol, half, left_side=True, lower=True, trans...  328 us
    all_gather x1, blocking collectives, per_device(): lax.all_gather(solved, ('sample', 'solver'), axis=0, tiled=True)  66.8 us
    another operation x14, matrix products, solve_group(): chol = jnp.linalg.cholesky(system)  58.6 us
    unnamed x71, local copies, waits for them, and re-layouts  43.7 us
    another operation x25, local copies, waits for them, and re-layouts  29.8 us
  transfers between devices with their start and end apart: 2, of which 1 were waited for; matrix products, arithmetic and copies ran while one was open for 7% of the time, Pallas kernels for 0%

commit v1 on v0

v1 whole, which is shorter than its diff:
```python
import functools

import jax
import jax.numpy as jnp
from jax import lax
from jax.experimental import pallas as pl
from jax.experimental.pallas import tpu as pltpu
from jax.sharding import PartitionSpec as P

SLICES = 128
CAP = 4
RIDGE = 2.0
LANES = 128
BLOCK = 16
MESH = pl.DeviceIdType.MESH
HIGHEST = lax.Precision.HIGHEST


def iota(shape, dim):
    return lax.broadcasted_iota(jnp.int32, shape, dim)


def one_hot(hit):
    return jnp.where(hit, 1.0, 0.0).astype(jnp.bfloat16)


def dot(a, b, dims=((1,), (0,)), precision=None):
    return lax.dot_general(
        a, b, (dims, ((), ())), precision=precision, preferred_element_type=jnp.float32
    )


def sweep(a, n):
    lane = iota((BLOCK, n), 1)
    sub = iota((BLOCK, n), 0)
    p = a[:BLOCK, :]
    for r in range(BLOCK):
        inv = 1.0 / p[r : r + 1, r : r + 1]
        col = p[:, r : r + 1]
        mod = jnp.where(lane == r, jnp.where(sub == r, 1.0, 0.0), p)
        row = mod[r : r + 1, :] * inv
        p = jnp.where(sub == r, row, mod - col * row)
    p = jnp.where(lane < BLOCK, -p, p)
    kept = jnp.where(iota(a.shape, 1) < BLOCK, 0.0, a)
    new = kept - dot(a[:, :BLOCK], p, precision=HIGHEST)
    new = jnp.concatenate([new[BLOCK:n], new[:BLOCK], new[n:]], axis=0)
    return pltpu.roll(new, n - BLOCK, 1)


def kernel(
    shape, oi, ids, obs, lf, lc, rc, rl, core_out, misfit_out,
    sbuf, rbuf, abuf, amat, send1, recv1, send2, recv2,
):
    n_solver, devices, owned, rows_per = shape
    count = oi.shape[1]
    rank = lf.shape[0]
    modes = lf.shape[1]
    n = devices * CAP
    me = lax.axis_index("sample") * n_solver + lax.axis_index("solver")

    def place(o):
        other = lax.rem(me + o, devices)
        return other, (other // n_solver, lax.rem(other, n_solver))

    barrier = pltpu.get_barrier_semaphore()

    def greet(o, c):
        pl.semaphore_signal(barrier, inc=1, device_id=place(o)[1], device_id_type=MESH)
        return c

    lax.fori_loop(1, devices, greet, 0)

    def hot(row):
        return one_hot(iota((modes, count), 0) == oi[row : row + 1, :])

    left = dot(lf[...], hot(0))
    right = dot(rl[...], hot(oi.shape[0] - 1))
    n_left, n_right = lc.shape[0], rc.shape[0]
    for level in range(max(n_left, n_right)):
        if level < n_left:
            picked = dot(lc[level], hot(level + 1)).reshape(rank, rank, count)
            left = jnp.sum(picked * left[:, None, :], axis=0)
        if level < n_right:
            at = n_right - 1 - level
            picked = dot(rc[at], hot(n_left + 1 + at)).reshape(rank, rank, count)
            right = jnp.sum(picked * right[None, :, :], axis=1)

    name = ids[...]
    same = one_hot(iota((SLICES, count), 0) == name)
    before = one_hot(iota((count, count), 0) < iota((count, count), 1))
    earlier = dot(same, before)
    slot = jnp.sum(
        jnp.where(iota((SLICES, count), 0) == name, earlier, 0.0), axis=0, keepdims=True
    ).astype(jnp.int32)
    owner = name // owned
    part = name - owner * owned
    spot = owner * rows_per + part * CAP + slot
    packed = jnp.concatenate(
        [
            left, right, jnp.broadcast_to(obs[...].astype(jnp.float32), (8, count)),
            jnp.zeros((LANES - 2 * rank - 8, count), jnp.float32),
        ],
        axis=0,
    ).astype(jnp.bfloat16)
    put = one_hot(iota((devices * rows_per, count), 0) == spot)
    sent = dot(put, packed, ((1,), (1,))).astype(jnp.bfloat16)
    sbuf[...] = sent.reshape(devices, rows_per, LANES)

    pl.semaphore_wait(barrier, devices - 1)

    def first(o):
        other, where = place(o)
        return pltpu.make_async_remote_copy(
            src_ref=sbuf.at[other], dst_ref=rbuf.at[me], send_sem=send1.at[o],
            recv_sem=recv1.at[o], device_id=where, device_id_type=MESH,
        )

    def start_first(o, c):
        first(o).start()
        return c

    def wait_first(o, c):
        first(o).wait()
        return c

    lax.fori_loop(1, devices, start_first, 0)
    rbuf[me] = sbuf[me]
    lax.fori_loop(1, devices, wait_first, 0)

    got = rbuf[...].reshape(devices * rows_per, LANES)
    spread = iota((LANES, rank * rank), 0)
    wide = iota((LANES, rank * rank), 1)
    spread_left = one_hot(spread == wide // rank)
    spread_right = one_hot(spread == rank + wide % rank)
    eye = jnp.where(iota((n, n), 0) == iota((n, n), 1), RIDGE, 0.0)
    order = iota((n, devices * rows_per), 0)
    source = iota((n, devices * rows_per), 1)
    rows = []
    for q in range(owned):
        pick = one_hot(source == (order // CAP) * rows_per + q * CAP + order % CAP)
        mine = dot(pick, got).astype(jnp.bfloat16)
        outer = (dot(mine, spread_left) * dot(mine, spread_right)).astype(jnp.bfloat16)
        rows.append(outer)
        amat[q, :n, :] = dot(outer, outer, ((1,), (1,))) + eye
        value = one_hot(iota((8, LANES), 1) == 2 * rank)
        amat[q, n:, :] = dot(value, mine, ((1,), (1,)))

    def step(t, c):
        for q in range(owned):
            amat[q] = sweep(amat[q], n)
        return c

    lax.fori_loop(0, n // BLOCK, step, 0)

    alphas = [amat[q, n : n + 1, :] for q in range(owned)]
    fill = [jnp.zeros((8 - owned, n), jnp.float32)] if owned < 8 else []
    abuf[me] = jnp.concatenate(alphas + fill, axis=0)

    def second(o):
        other, where = place(o)
        return pltpu.make_async_remote_copy(
            src_ref=abuf.at[me], dst_ref=abuf.at[me], send_sem=send2.at[o],
            recv_sem=recv2.at[o], device_id=where, device_id_type=MESH,
        )

    def start_second(o, c):
        second(o).start()
        return c

    def wait_second(o, c):
        second(o).wait()
        return c

    lax.fori_loop(1, devices, start_second, 0)
    for q in range(owned):
        alpha = jnp.broadcast_to(alphas[q], (8, n))
        core_out[q : q + 1, :] = dot(alpha, rows[q].astype(jnp.float32), precision=HIGHEST)[:1]
    lax.fori_loop(1, devices, wait_second, 0)

    table = abuf[...].reshape(devices * 8, n)
    from_row = owner * 8 + part
    pick = jnp.where(iota((devices * 8, count), 0) == from_row, 1.0, 0.0)
    lanes = dot(table, pick, ((0,), (0,)), precision=HIGHEST)
    chosen = jnp.where(iota((n, count), 0) == me * CAP + slot, lanes, 0.0)
    misfit_out[...] = RIDGE * jnp.sum(chosen, axis=0, keepdims=True)


def per_device(shape, other_index, slice_index, observed, left_first, left_cores, right_cores, right_last):
    n_solver, devices, owned, rows_per = shape
    rank = left_first.shape[1]
    modes = left_first.shape[0]
    count = observed.shape[0]
    n = devices * CAP

    def flat(cores):
        return jnp.transpose(cores, (0, 2, 3, 1)).reshape(cores.shape[0], rank * rank, modes)

    core, misfit = pl.pallas_call(
        functools.partial(kernel, shape),
        out_shape=(
            jax.ShapeDtypeStruct((owned, rank * rank), jnp.float32),
            jax.ShapeDtypeStruct((1, count), jnp.float32),
        ),
        in_specs=[pl.BlockSpec(memory_space=pltpu.VMEM)] * 7,
        out_specs=(pl.BlockSpec(memory_space=pltpu.VMEM),) * 2,
        scratch_shapes=[
            pltpu.VMEM((devices, rows_per, LANES), jnp.bfloat16),
            pltpu.VMEM((devices, rows_per, LANES), jnp.bfloat16),
            pltpu.VMEM((devices, 8, n), jnp.float32),
            pltpu.VMEM((owned, n + 8, n), jnp.float32),
            pltpu.SemaphoreType.DMA((devices,)),
            pltpu.SemaphoreType.DMA((devices,)),
            pltpu.SemaphoreType.DMA((devices,)),
            pltpu.SemaphoreType.DMA((devices,)),
        ],
        compiler_params=pltpu.CompilerParams(
            collective_id=0, has_side_effects=True, vmem_limit_bytes=48 * 1024 * 1024
        ),
    )(
        other_index, slice_index.reshape(1, count), observed.reshape(1, count), left_first.T,
        flat(left_cores), flat(right_cores), right_last.T,
    )
    return core, misfit.reshape(count)


def solution(mesh):
    n_solver = mesh.shape["solver"]
    devices = mesh.shape["sample"] * n_solver
    owned = SLICES // devices
    rows_per = -(-owned * CAP // 16) * 16
    both = ("sample", "solver")
    return jax.shard_map(
        functools.partial(per_device, (n_solver, devices, owned, rows_per)),
        mesh=mesh,
        in_specs=(P(None, both), P(both, None), P(both), P(), P(), P(), P()),
        out_specs=(P(both, None), P(both)),
        check_vma=False,
    )
```

time: 1420 us -> 47.2 us (0.03)
  other arithmetic: 1030 us -> 0 us
  local copies, waits for them, and re-layouts: 150 us -> 7.99 us
  matrix products: 132 us -> 0 us
  blocking collectives: 66.8 us -> 0 us
  Pallas kernels: 0 us -> 38.1 us
  waiting for transfers between devices: 21.3 us -> 0 us
    another operation x57 -> x0, other arithmetic: 1000 us -> none  [the longest x34 672 us: solve_group(): chol = jnp.linalg.cholesky(system)]
    another operation x44 -> x0, matrix products: 95.7 us -> none  [the longest x14 58.6 us: solve_group(): chol = jnp.linalg.cholesky(system)]
    all_gather x1 -> x0, blocking collectives: 66.8 us -> none  [per_device(): lax.all_gather(solved, ('sample', 'solver'), axis=0, tiled=True)]
    another operation x41 -> x0, local copies, waits for them, and re-layouts: 42 us -> none
    pallas_call x0 -> x1, Pallas kernels: none -> 38.1 us  [per_device(): pl.pallas_call(functools.partial(kernel, shape), out_shape=(jax.ShapeDtyp...]
    unnamed x71 -> x14, local copies, waits for them, and re-layouts: 43.7 us -> 7.33 us
    dot_general x11 -> x0, matrix products: 36.2 us -> none  [the longest x5 16.3 us: interfaces(): jnp.einsum('ejk,ek->ej', mats, right, precision=lax.Precision.HIGHEST, pr...]
    gather x14 -> x0, local copies, waits for them, and re-layouts: 34.8 us -> none  [the longest x5 16.1 us: interfaces(): jnp.take(right_cores[level], index_block[count_left + 1 + level], axis=0)]
  transfers between devices with their start and end apart: 2 -> 0, of which waited for: 1 -> 0; matrix products, arithmetic and copies ran while one was open for 7% -> 0% of each run, Pallas kernels for 0% -> 0%
where the time goes in v1:
time: 47.2 us; the launch traced here: 46.7 us
  Pallas kernels  38.1 us (81%)
  local copies, waits for them, and re-layouts  7.99 us (17%)
  between operations  0.64 us (1%)
    pallas_call x1, Pallas kernels, per_device(): pl.pallas_call(functools.partial(kernel, shape), out_shape=(jax.ShapeDtyp...  38.1 us
    unnamed x14, local copies, waits for them, and re-layouts  7.33 us

profile of v1, /device:TPU:0, one launch (start us, length us, event | category | flops | bytes accessed | tf_op | source)
XLA Modules:
  0.0 46.7 jit_solution(9225358281835026)
XLA Ops:
  0.6 0.7 %reshape.20.obs = bf16[1,256]{1,0:T(2,128)(2,1)S(1)} reshape(bf16[256]{0:T(256)(128)(2,1)} %param.9) | data formatting | bytes 1024 | tf_op jit(solution)/shard_map/reshape | solution.py:220
  1.3 0.0 copy-start
  1.3 1.7 %copy-done = bf16[5,256,32,32]{1,3,2,0:T(8,128)(2,1)S(1)} copy-done((bf16[5,256,32,32]{1,3,2,0:T(8,128)(2,1)S(1)}, bf16[5,256,32,32]{1,3,2,0:T(8,128)(2,1)}, u32[]{:S(2)}) %copy-start) | copy-done | bytes 2621464
  3.0 0.0 copy-start.1
  3.0 1.6 %copy-done.1 = bf16[4,256,32,32]{1,3,2,0:T(8,128)(2,1)S(1)} copy-done((bf16[4,256,32,32]{1,3,2,0:T(8,128)(2,1)S(1)}, bf16[4,256,32,32]{1,3,2,0:T(8,128)(2,1)}, u32[]{:S(2)}) %copy-start.1) | copy-done | bytes 2097176
  4.6 0.0 copy-start.2
  4.6 0.7 %copy-done.2 = s32[11,256]{1,0:T(8,128)S(1)} copy-done((s32[11,256]{1,0:T(8,128)S(1)}, s32[11,256]{1,0:T(8,128)}, u32[]{:S(2)}) %copy-start.2) | copy-done | bytes 11288
  5.3 0.0 copy-start.3
  5.3 0.7 %copy-done.3 = bf16[256,32]{0,1:T(8,128)(2,1)S(1)} copy-done((bf16[256,32]{0,1:T(8,128)(2,1)S(1)}, bf16[256,32]{0,1:T(8,128)(2,1)}, u32[]{:S(2)}) %copy-start.3) | copy-done | bytes 16408
  6.1 0.0 copy-start.4
  6.1 0.7 %copy-done.4 = bf16[256,32]{0,1:T(8,128)(2,1)S(1)} copy-done((bf16[256,32]{0,1:T(8,128)(2,1)S(1)}, bf16[256,32]{0,1:T(8,128)(2,1)}, u32[]{:S(2)}) %copy-start.4) | copy-done | bytes 16408
  6.8 0.0 copy-start.5
  6.8 0.7 %copy-done.5 = s32[256,1]{0,1:T(1,128)S(1)} copy-done((s32[256,1]{0,1:T(1,128)S(1)}, s32[256,1]{0,1:T(1,128)}, u32[]{:S(2)}) %copy-start.5) | copy-done | bytes 1048
  7.5 38.1 %shard_map.86 = (f32[4,1024]{1,0:T(4,128)S(1)}, f32[1,256]{1,0:T(1,128)S(1)}) custom-call(s32[11,256]{1,0:T(8,128)S(1)} %copy-done.2, s32[1,256]{1,0:T(1,128)S(1)} %bitcast.14, bf16[1,256]{1,0:T(2,128)(2,1)S(1)} %reshape.20.obs, bf16[32,256]{1,0:T(8,128)(2,1)S(1)} %bitcast.12, bf16[4,1024,256]{2,1,0:T(8,128)(2,1)S(1)} %bitcast.11, ...), custom_call_target="tpu_custom_call" | custom-call | tf_op jit(solution)/shard_map/pallas_call | solution.py:198
  45.5 0.6 %copy.11 = f32[4,1024]{1,0:T(4,128)} copy(f32[4,1024]{1,0:T(4,128)S(1)} %get-tuple-element.8) | data formatting | bytes 32768
  46.1 0.6 %copy.12 = f32[256]{0:T(256)} copy(f32[256]{0:T(256)S(1)} %bitcast.15) | data formatting | bytes 2048
Async XLA Ops:
  1.3 1.7 %copy-start = (bf16[5,256,32,32]{1,3,2,0:T(8,128)(2,1)S(1)}, bf16[5,256,32,32]{1,3,2,0:T(8,128)(2,1)}, u32[]{:S(2)}) copy-start(bf16[5,256,32,32]{1,3,2,0:T(8,128)(2,1)} %param.12) | copy-start | bytes 7864324
  3.0 1.6 %copy-start.1 = (bf16[4,256,32,32]{1,3,2,0:T(8,128)(2,1)S(1)}, bf16[4,256,32,32]{1,3,2,0:T(8,128)(2,1)}, u32[]{:S(2)}) copy-start(bf16[4,256,32,32]{1,3,2,0:T(8,128)(2,1)} %param.11) | copy-start | bytes 6291460
  4.6 0.7 %copy-start.2 = (s32[11,256]{1,0:T(8,128)S(1)}, s32[11,256]{1,0:T(8,128)}, u32[]{:S(2)}) copy-start(s32[11,256]{1,0:T(8,128)} %oi.1) | copy-start | bytes 33796
  5.3 0.7 %copy-start.3 = (bf16[256,32]{0,1:T(8,128)(2,1)S(1)}, bf16[256,32]{0,1:T(8,128)(2,1)}, u32[]{:S(2)}) copy-start(bf16[256,32]{0,1:T(8,128)(2,1)} %param.10) | copy-start | bytes 49156
  6.1 0.7 %copy-start.4 = (bf16[256,32]{0,1:T(8,128)(2,1)S(1)}, bf16[256,32]{0,1:T(8,128)(2,1)}, u32[]{:S(2)}) copy-start(bf16[256,32]{0,1:T(8,128)(2,1)} %param.13) | copy-start | bytes 49156
  6.8 0.7 %copy-start.5 = (s32[256,1]{0,1:T(1,128)S(1)}, s32[256,1]{0,1:T(1,128)}, u32[]{:S(2)}) copy-start(s32[256,1]{0,1:T(1,128)} %param.8) | copy-start | bytes 3076

commit v2 on v1

--- a/solution.py
+++ b/solution.py
@@ -30,26 +30,50 @@
     )
 
 
+def split3(x):
+    first = x.astype(jnp.bfloat16)
+    rest = x - first.astype(jnp.float32)
+    second = rest.astype(jnp.bfloat16)
+    third = (rest - second.astype(jnp.float32)).astype(jnp.bfloat16)
+    return first, second, third
+
+
+def update(a, p):
+    a1, a2, a3 = split3(a[:, :BLOCK])
+    p1, p2, p3 = split3(p)
+    return dot(
+        jnp.concatenate([a1, a1, a2, a2, a1, a3], axis=1),
+        jnp.concatenate([p1, p2, p1, p2, p3, p1], axis=0),
+    )
+
+
 def sweep(a, n):
     lane = iota((BLOCK, n), 1)
     sub = iota((BLOCK, n), 0)
     p = a[:BLOCK, :]
-    for r in range(BLOCK):
-        inv = 1.0 / p[r : r + 1, r : r + 1]
-        col = p[:, r : r + 1]
+    for r in range(0, BLOCK, 2):
+        c0 = jnp.broadcast_to(p[:, r : r + 1], p.shape)
+        c1 = jnp.broadcast_to(p[:, r + 1 : r + 2], p.shape)
         mod = jnp.where(lane == r, jnp.where(sub == r, 1.0, 0.0), p)
-        row = mod[r : r + 1, :] * inv
-        p = jnp.where(sub == r, row, mod - col * row)
+        mod = jnp.where(lane == r + 1, jnp.where(sub == r + 1, 1.0, 0.0), mod)
+        inv0 = 1.0 / c0[r : r + 1, :]
+        ratio = c0[r + 1 : r + 2, :] * inv0
+        inv1 = 1.0 / (c1[r + 1 : r + 2, :] - ratio * c1[r : r + 1, :])
+        m0, m1 = mod[r : r + 1, :], mod[r + 1 : r + 2, :]
+        row1 = (m1 - ratio * m0) * inv1
+        row0 = m0 * inv0 - (c1[r : r + 1, :] * inv0) * row1
+        p = jnp.where(sub == r, row0, jnp.where(sub == r + 1, row1, mod - c0 * row0 - c1 * row1))
     p = jnp.where(lane < BLOCK, -p, p)
     kept = jnp.where(iota(a.shape, 1) < BLOCK, 0.0, a)
-    new = kept - dot(a[:, :BLOCK], p, precision=HIGHEST)
+    new = kept - update(a, p)
     new = jnp.concatenate([new[BLOCK:n], new[:BLOCK], new[n:]], axis=0)
     return pltpu.roll(new, n - BLOCK, 1)
 
 
 def kernel(
-    shape, oi, ids, obs, lf, lc, rc, rl, core_out, misfit_out,
-    sbuf, rbuf, abuf, amat, send1, recv1, send2, recv2,
+    shape, oi_hbm, ids_hbm, obs_hbm, lf_hbm, lc_hbm, rc_hbm, rl_hbm, core_out, misfit_out,
+    oi, ids, obs, lf, lc, rc, rl, sbuf, rbuf, sbuf2, rbuf2, amat,
+    load_small, load_left, load_right, send1, recv1, send2, recv2,
 ):
     n_solver, devices, owned, rows_per = shape
     count = oi.shape[1]
@@ -68,20 +92,39 @@
         pl.semaphore_signal(barrier, inc=1, device_id=place(o)[1], device_id_type=MESH)
         return c
 
+    small = [
+        pltpu.make_async_copy(a, b, load_small.at[i])
+        for i, (a, b) in enumerate(
+            ((oi_hbm, oi), (lf_hbm, lf), (rl_hbm, rl), (ids_hbm, ids), (obs_hbm, obs))
+        )
+    ]
+    n_left, n_right = lc.shape[0], rc.shape[0]
+    lefts = [pltpu.make_async_copy(lc_hbm.at[i], lc.at[i], load_left.at[i]) for i in range(n_left)]
+    rights = [pltpu.make_async_copy(rc_hbm.at[i], rc.at[i], load_right.at[i]) for i in range(n_right)]
+    for copy in small:
+        copy.start()
+    for level in range(max(n_left, n_right)):
+        if level < n_left:
+            lefts[level].start()
+        if level < n_right:
+            rights[n_right - 1 - level].start()
     lax.fori_loop(1, devices, greet, 0)
+    for copy in small:
+        copy.wait()
 
     def hot(row):
         return one_hot(iota((modes, count), 0) == oi[row : row + 1, :])
 
     left = dot(lf[...], hot(0))
     right = dot(rl[...], hot(oi.shape[0] - 1))
-    n_left, n_right = lc.shape[0], rc.shape[0]
     for level in range(max(n_left, n_right)):
         if level < n_left:
+            lefts[level].wait()
             picked = dot(lc[level], hot(level + 1)).reshape(rank, rank, count)
             left = jnp.sum(picked * left[:, None, :], axis=0)
         if level < n_right:
             at = n_right - 1 - level
+            rights[at].wait()
             picked = dot(rc[at], hot(n_left + 1 + at)).reshape(rank, rank, count)
             right = jnp.sum(picked * right[None, :, :], axis=1)
 
@@ -153,13 +196,21 @@
     lax.fori_loop(0, n // BLOCK, step, 0)
 
     alphas = [amat[q, n : n + 1, :] for q in range(owned)]
-    fill = [jnp.zeros((8 - owned, n), jnp.float32)] if owned < 8 else []
-    abuf[me] = jnp.concatenate(alphas + fill, axis=0)
+    mine_of = iota((devices, n), 1) // CAP == iota((devices, n), 0)
+    answers = jnp.zeros((devices, LANES), jnp.float32)
+    for q in range(owned):
+        to = iota((n, LANES), 1) == q * CAP + iota((n, LANES), 0) % CAP
+        answers += dot(
+            jnp.where(mine_of, alphas[q], 0.0), jnp.where(to, 1.0, 0.0), precision=HIGHEST
+        )
+    for d in range(devices):
+        sbuf2[d, 0:1, :] = answers[d : d + 1, :]
+    rbuf2[me] = sbuf2[me]
 
     def second(o):
         other, where = place(o)
         return pltpu.make_async_remote_copy(
-            src_ref=abuf.at[me], dst_ref=abuf.at[me], send_sem=send2.at[o],
+            src_ref=sbuf2.at[other], dst_ref=rbuf2.at[me], send_sem=send2.at[o],
             recv_sem=recv2.at[o], device_id=where, device_id_type=MESH,
         )
 
@@ -177,11 +228,10 @@
         core_out[q : q + 1, :] = dot(alpha, rows[q].astype(jnp.float32), precision=HIGHEST)[:1]
     lax.fori_loop(1, devices, wait_second, 0)
 
-    table = abuf[...].reshape(devices * 8, n)
-    from_row = owner * 8 + part
-    pick = jnp.where(iota((devices * 8, count), 0) == from_row, 1.0, 0.0)
+    table = jnp.concatenate([rbuf2[d] for d in range(devices)], axis=0)
+    pick = jnp.where(iota((devices, count), 0) == owner, 1.0, 0.0)
     lanes = dot(table, pick, ((0,), (0,)), precision=HIGHEST)
-    chosen = jnp.where(iota((n, count), 0) == me * CAP + slot, lanes, 0.0)
+    chosen = jnp.where(iota((LANES, count), 0) == part * CAP + slot, lanes, 0.0)
     misfit_out[...] = RIDGE * jnp.sum(chosen, axis=0, keepdims=True)
 
 
@@ -201,20 +251,31 @@
             jax.ShapeDtypeStruct((owned, rank * rank), jnp.float32),
             jax.ShapeDtypeStruct((1, count), jnp.float32),
         ),
-        in_specs=[pl.BlockSpec(memory_space=pltpu.VMEM)] * 7,
+        in_specs=[pl.BlockSpec(memory_space=pltpu.HBM)] * 7,
         out_specs=(pl.BlockSpec(memory_space=pltpu.VMEM),) * 2,
         scratch_shapes=[
+            pltpu.VMEM(other_index.shape, jnp.int32),
+            pltpu.VMEM((1, count), jnp.int32),
+            pltpu.VMEM((1, count), jnp.bfloat16),
+            pltpu.VMEM((rank, modes), jnp.bfloat16),
+            pltpu.VMEM((left_cores.shape[0], rank * rank, modes), jnp.bfloat16),
+            pltpu.VMEM((right_cores.shape[0], rank * rank, modes), jnp.bfloat16),
+            pltpu.VMEM((rank, modes), jnp.bfloat16),
             pltpu.VMEM((devices, rows_per, LANES), jnp.bfloat16),
             pltpu.VMEM((devices, rows_per, LANES), jnp.bfloat16),
-            pltpu.VMEM((devices, 8, n), jnp.float32),
+            pltpu.VMEM((devices, 1, LANES), jnp.float32),
+            pltpu.VMEM((devices, 1, LANES), jnp.float32),
             pltpu.VMEM((owned, n + 8, n), jnp.float32),
+            pltpu.SemaphoreType.DMA((5,)),
+            pltpu.SemaphoreType.DMA((left_cores.shape[0],)),
+            pltpu.SemaphoreType.DMA((right_cores.shape[0],)),
             pltpu.SemaphoreType.DMA((devices,)),
             pltpu.SemaphoreType.DMA((devices,)),
             pltpu.SemaphoreType.DMA((devices,)),
             pltpu.SemaphoreType.DMA((devices,)),
         ],
         compiler_params=pltpu.CompilerParams(
-            collective_id=0, has_side_effects=True, vmem_limit_bytes=48 * 1024 * 1024
+            collective_id=0, has_side_effects=True, vmem_limit_bytes=60 * 1024 * 1024
         ),
     )(
         other_index, slice_index.reshape(1, count), observed.reshape(1, count), left_first.T,

time: 47.2 us -> 38.1 us (0.81)
  Pallas kernels: 38.1 us -> 33.3 us
  local copies, waits for them, and re-layouts: 7.99 us -> 3.76 us
    unnamed x14 -> x2, local copies, waits for them, and re-layouts: 7.33 us -> 2.54 us
    pallas_call x1, Pallas kernels: 38.1 us -> 33.3 us  [per_device(): pl.pallas_call(functools.partial(kernel, shape), out_shape=(jax.ShapeDtyp...]
    reshape x1, local copies, waits for them, and re-layouts: 0.66 us -> 1.22 us  [per_device(): observed.reshape(1, count)]
where the time goes in v2:
time: 38.1 us; the launch traced here: 37.7 us
  Pallas kernels  33.3 us (87%)
  local copies, waits for them, and re-layouts  3.76 us (10%)
  between operations  0.64 us (2%)
    pallas_call x1, Pallas kernels, per_device(): pl.pallas_call(functools.partial(kernel, shape), out_shape=(jax.ShapeDtyp...  33.3 us
    unnamed x2, local copies, waits for them, and re-layouts  2.54 us
    reshape x1, local copies, waits for them, and re-layouts, per_device(): observed.reshape(1, count)  1.22 us

profile of v2, /device:TPU:0, one launch (start us, length us, event | category | flops | bytes accessed | tf_op | source)
XLA Modules:
  0.0 37.7 jit_solution(6585311039301705038)
XLA Ops:
  0.6 1.2 %reshape.20.obs_hbm = bf16[1,256]{1,0:T(2,128)(2,1)} reshape(bf16[256]{0:T(256)(128)(2,1)} %param.9) | data formatting | bytes 1024 | tf_op jit(solution)/shard_map/reshape | solution.py:281
  1.9 33.3 %shard_map.86 = (f32[4,1024]{1,0:T(4,128)}, f32[1,256]{1,0:T(1,128)}) custom-call(s32[11,256]{1,0:T(8,128)} %oi_hbm.1, s32[1,256]{1,0:T(1,128)} %bitcast.14, bf16[1,256]{1,0:T(2,128)(2,1)} %reshape.20.obs_hbm, bf16[32,256]{1,0:T(8,128)(2,1)} %bitcast.12, bf16[4,1024,256]{2,1,0:T(8,128)(2,1)} %bitcast.11, bf16[5,1024,256]{2,1,0:T(8,128)(2,1)} %bitcast.10, ...), custom_call_target="tpu_custom_call" | custom-call | tf_op jit(solution)/shard_map/pallas_call | solution.py:248
  35.2 1.3 %copy.11 = f32[4,1024]{1,0:T(4,128)} copy(f32[4,1024]{1,0:T(4,128)} %get-tuple-element.8) | data formatting | bytes 32768
  36.5 1.2 %copy.12 = f32[256]{0:T(256)} copy(f32[256]{0:T(256)} %bitcast.15) | data formatting | bytes 2048
